TPU v7x, 32 devices: a whole 2x2x4 slice. The times are simulated.
32 devices in a mesh: patch: 8 (over z, y), level: 4 (over x, core).
Axes of the slice: x: 2, y: 2, z: 4, core: 2. Of those that a mesh axis runs over, the one named last changes fastest.
Arguments:
- fields: float32 [6, 64, 8192], P(None, None, ('patch', 'level')), may hold values from -6 to 6
- inv_jacobian: float32 [8192], P(('patch', 'level')), may hold values from 0.5 to 2
- diff_matrix: float32 [3, 64, 64], replicated, may hold values from -0.75 to 0.75
- face_interp: float32 [6, 16, 64], replicated, may hold values from -0.75 to 0.75
- lift_matrix: float32 [6, 64, 16], replicated, may hold values from -1.5 to 1.5
- flux_couple: float32 [6, 6, 6], replicated, may hold values from -2.5 to 2.5
- neighbours: int32 [6, 8192], P(None, ('patch', 'level')), may hold values from 0 to 287
- send_index: int32 [2, 512], P(None, ('patch', 'level')), may hold values from 0 to 255
- bound_coef: float32 [6], replicated, may hold values from 0.5 to 1.5
- current_coef: float32 [6], replicated, may hold values from -1 to 1
- time_interp: float32 [64], replicated, may hold values from -2 to 2
- current_history: bfloat16 [64, 4096], P(None, ('patch', 'level')), may hold values from -6 to 6
- group_weight: bfloat16 [32, 4096], P(None, ('patch', 'level')), may hold values from -0.1875 to 0.1875
- projection: bfloat16 [4096, 512], P(('patch', 'level')), may hold values from -6 to 6
- kernels: bfloat16 [4, 8, 4, 64], P('level', 'patch'), may hold values from -0.75 to 0.75
- pair_dest: int32 [4, 8, 4], P('level', 'patch'), may hold values from 0 to 7, as said below
- pair_count: int32 [4, 8], P('level', 'patch'), may hold values from 2 to 4
Outputs:
- field_rate: float32 [6, 64, 8192], P(None, None, ('patch', 'level'))
- boundary_field: float32 [64, 4096], P(None, ('patch', 'level'))
Inputs may be any that keep to these rules, and one draw needn't show every extreme that they name: `pair_dest`: in each row the 4 entries are distinct patches, none the row's own patch. Only the first pair_count slots of a group are live. `neighbours`: indices below 256 are the device's own elements, then 16 ghosts from the device below and 16 from the device above along patch+level, wrapping. `send_index`: local element indices of the device.
All inputs are finite; a program needn't handle non-finite values.
Results may differ from a plain program's by a relative error of at most 0.0049.
Values may be sent and summed in bfloat16 or wider, within the bound.
A program may use at most 192 MiB of HBM per device.

v0:
```python
import jax
import jax.numpy as jnp
from jax import lax
from jax.sharding import PartitionSpec as P

NFP = 16
BE = 8


HIGH = lax.Precision.HIGHEST


def padded_2(array, sides, width):
    for axis, dim in sides:
        size, length = (lax.axis_size(axis), array.shape[dim])
        up = [(i, (i + 1) % size) for i in range(size)]
        down = [(j, i) for i, j in up]
        last = lax.slice_in_dim(array, length - width, length, axis=dim)
        leading = lax.slice_in_dim(array, 0, width, axis=dim)
        before = lax.ppermute(last, axis, up)
        after = lax.ppermute(leading, axis, down)
        array = jnp.concatenate([before, array, after], axis=dim)
    return array


def toeplitz(rows):
    count = rows.shape[-1]
    lagged = jnp.arange(count)[:, None] - jnp.arange(count)[None, :]
    picked = jnp.take(rows, jnp.clip(lagged, 0, count - 1), axis=-1)
    return jnp.where(lagged >= 0, picked, jnp.zeros_like(picked))


def per_device(
    fields,
    inv_jacobian,
    diff_matrix,
    face_interp,
    lift_matrix,
    flux_couple,
    neighbours,
    send_index,
    bound_coef,
    current_coef,
    time_interp,
    current_history,
    group_weight,
    projection,
    kernels,
    pair_dest,
    pair_count,
):
    elements = fields.shape[2]
    listed = send_index.shape[1]
    directions = projection.shape[1]
    packed = jnp.take(fields, send_index.reshape(-1), axis=2)
    extended = padded_2(packed.astype(jnp.bfloat16), ((("patch", "level"), 2),), listed).astype(
        packed.dtype
    )
    own = jnp.einsum("fqn,cne->fcqe", face_interp, fields, precision=HIGH)
    newest = jnp.einsum("c,cqe->eq", current_coef, own[5, :, :, :BE], precision=HIGH)
    newest = newest.reshape(1, -1).astype(jnp.bfloat16)
    currents = jnp.concatenate([current_history[1:], newest], axis=0)
    grads = jnp.einsum("rmn,cne->rcme", diff_matrix, fields, precision=HIGH) * inv_jacobian
    electric = jnp.stack(
        [grads[1, 5] - grads[2, 4], grads[2, 3] - grads[0, 5], grads[0, 4] - grads[1, 3]]
    )
    magnetic = -jnp.stack(
        [grads[1, 2] - grads[2, 1], grads[2, 0] - grads[0, 2], grads[0, 1] - grads[1, 0]]
    )
    volume = jnp.concatenate([electric, magnetic], axis=0)
    owner = lax.axis_index("patch") * lax.axis_size("level") + lax.axis_index("level")
    shard_currents = lax.all_gather(currents[None], ("patch", "level"), axis=0, tiled=True)
    shard_weights = lax.all_gather(group_weight[None], ("patch", "level"), axis=0, tiled=True)
    shard_projection = lax.all_gather(projection[None], ("patch", "level"), axis=0, tiled=True)
    row = lax.dynamic_index_in_dim(shard_weights, owner, 1, keepdims=False)
    weighted = (shard_currents.astype(jnp.float32) * row.astype(jnp.float32)[:, None, :]).astype(
        jnp.bfloat16
    )
    rays = jnp.einsum("ntb,nbk->tk", weighted, shard_projection, preferred_element_type=jnp.float32)
    rays = rays.astype(jnp.bfloat16)
    patches = lax.axis_size("patch")
    pairs = pair_dest.shape[2]
    live = jnp.arange(pairs) < pair_count[0, 0]
    slots = (pair_dest[0, 0][None, :] == jnp.arange(patches)[:, None]) & live[None, :]
    table = jnp.dot(
        slots.astype(jnp.float32), kernels[0, 0].astype(jnp.float32), precision=HIGH
    ).astype(jnp.bfloat16)
    blocks = jnp.einsum("dts,sk->dtk", toeplitz(table), rays, preferred_element_type=jnp.float32)
    received = lax.all_to_all(blocks, "patch", split_axis=0, concat_axis=0, tiled=True)
    incoming = jnp.sum(received, axis=0)
    incoming = incoming.astype(jnp.bfloat16)
    image = jnp.einsum(
        "ntk,bk->ntb",
        lax.all_gather(incoming[None], ("patch", "level"), axis=0, tiled=True),
        projection,
        preferred_element_type=jnp.float32,
    )
    boundary_field = jnp.einsum(
        "ntb,nb->tb", image, group_weight.astype(jnp.float32), precision=HIGH
    )
    boundary_field = boundary_field * (1.0 / jnp.sqrt(jnp.float32(directions)))
    ghosts = jnp.concatenate([extended[:, :, :listed], extended[:, :, 3 * listed :]], axis=2)
    pool = jnp.concatenate([fields, ghosts], axis=2)
    opposite = face_interp[jnp.array([1, 0, 3, 2, 5, 4])]
    across = pool[:, :, neighbours]
    neighbour = jnp.einsum("fqn,cnfe->fcqe", opposite, across, precision=HIGH)
    interp = jnp.dot(time_interp, boundary_field, precision=HIGH).reshape(BE, NFP)
    exterior = bound_coef[:, None, None] * interp.T[None]
    padded = jnp.pad(exterior, ((0, 0), (0, 0), (0, elements - BE)))
    isbound = (jnp.arange(6)[:, None, None, None] == 5) & (
        jnp.arange(elements)[None, None, None, :] < BE
    )
    neighbour = jnp.where(isbound, padded[None], neighbour)
    flux = jnp.einsum("fcd,fdqe->fcqe", flux_couple, neighbour - own, precision=HIGH)
    surface = jnp.einsum("fnq,fcqe->cne", lift_matrix, flux, precision=HIGH)
    return (volume + surface, boundary_field)


def solution(mesh):
    placed = (
        P(None, None, ("patch", "level")),
        P(("patch", "level")),
        P(),
        P(),
        P(),
        P(),
        P(None, ("patch", "level")),
        P(None, ("patch", "level")),
        P(),
        P(),
        P(),
        P(None, ("patch", "level")),
        P(None, ("patch", "level")),
        P(("patch", "level"), None),
        P("level", "patch", None, None),
        P("level", "patch", None),
        P("level", "patch"),
    )
    return jax.shard_map(
        per_device,
        mesh=mesh,
        in_specs=placed,
        out_specs=(P(None, None, ("patch", "level")), P(None, ("patch", "level"))),
        check_vma=False,
    )
```

profile of v0, /device:TPU:0, one launch (start us, length us, event | category | flops | bytes accessed | tf_op | source)
XLA Modules:
  0.0 216.3 jit_solution(4108628753665662777)
XLA Ops:
  7.2 0.7 all-gather.7.cloned.1.call-update
  8.6 0.8 convolution_convert_fusion
  9.5 0.1 copy.43
  9.6 0.7 slice.66
  10.4 1.6 convolution_bitcast_fusion.1
  12.0 0.7 fusion.51
  12.7 0.1 copy.53
  12.8 0.1 convert_element_type.58
  12.9 12.1 %gather_fusion = bf16[4096,8]{1,0:T(8,128)(2,1)S(1)} fusion(bf16[8,64]{0,1:T(8,128)(2,1)S(1)} %copy.43, s32[4096]{0:T(1024)S(1)} %broadcast_clamp_fusion), kind=kCustom, calls=%fused_computation | custom fusion | bytes 147456 | tf_op jit(solution)/shard_map/jit(_take)/gather | solution.py:29
  25.0 0.4 copy.44
  25.5 44.3 %all-gather.1 = bf16[1024,128]{1,0:T(8,128)(2,1)S(1)} all-gather(bf16[32,128]{1,0:T(8,128)(2,1)S(1)} %copy-done.6), channel_id=3, replica_groups=mesh['patch'=8,'level'=4] {'patch','level'}, dimensions={0}, use_global_device_ids=true | all-gather | bytes 270336 | tf_op jit(solution)/shard_map/all_gather | solution.py:73
  69.8 38.2 %all-gather = bf16[2048,128]{1,0:T(8,128)(2,1)S(1)} all-gather(bf16[64,128]{1,0:T(8,128)(2,1)S(1)} %pad_maximum_fusion.3), channel_id=2, replica_groups=mesh['patch'=8,'level'=4] {'patch','level'}, dimensions={0}, use_global_device_ids=true | all-gather | bytes 540672 | tf_op jit(solution)/shard_map/all_gather | solution.py:72
  108.0 3.2 %fusion.18 = f32[8,64,512]{2,1,0:T(8,128)S(1)} fusion(bf16[32,128,512]{2,1,0:T(8,128)(2,1)} %bitcast.176, bf16[32,64,128]{2,1,0:T(8,128)(2,1)S(1)} %bitcast.177, f32[32,128]{1,0:T(8,128)S(1)} %bitcast.180, bf16[64,64,8]{1,0,2:T(8,128)(2,1)S(1)} %copy.44, pred[64,64]{1,0:T(8,128)(4,1)S(1)} %get-tuple-element.11, pred[64,64]{1,0:T(8,128)(4,1)S(1)} %get-tuple-element.12), kind=kOutput, calls=%fused_computation.25 | convolution fusion | flops 302874624 | bytes 5857280 | tf_op jit(solution)/shard_map/dts,sk->dtk/dot_general | solution.py:88
  111.3 29.1 %all_to_all.5 = f32[8,64,512]{2,1,0:T(8,128)S(1)} all-to-all(f32[8,64,512]{2,1,0:T(8,128)S(1)} %fusion.18), channel_id=1, replica_groups=mesh['patch'=8,'level'=4] {'patch'}, dimensions={0} | all-to-all | bytes 2097152 | tf_op jit(solution)/shard_map/all_to_all | solution.py:89
  140.4 0.7 reduce_sum.9
  141.1 0.1 reshape.269
  141.2 0.1 reshape.268
  141.3 0.4 copy.47
  141.8 0.6 gather_fusion.1
  142.4 0.1 fusion.36
  142.6 5.3 %collective-permute-start.1 = (bf16[6,64,16]{1,0,2:T(8,128)(2,1)S(1)}, bf16[6,64,16]{1,0,2:T(8,128)(2,1)S(1)}, u32[]{:S(2)}, u32[]{:S(2)}) collective-permute-start(bf16[6,64,16]{1,0,2:T(8,128)(2,1)S(1)} %get-tuple-element.10), channel_id=1, source_target_pairs={{1,0},{2,1},{3,2},{4,3},{5,4},{6,5},{7,6},{8,7},{9,8},{10,9},{11,1... | collective-permute-start | bytes 36872 | tf_op jit(solution)/shard_map/ppermute | solution.py:21
  147.9 1.1 fusion.2
  149.2 0.6 gather_fusion.3
  149.9 0.2 pad_maximum_fusion
  150.0 5.7 %gather_fusion.2 = f32[1536,6,64]{2,1,0:T(8,128)} fusion(f32[6,64,288]{1,0,2:T(8,128)S(1)} %pad_maximum_fusion, s32[2048]{0:T(1024)S(1)} %pad_clamp_fusion), kind=kCustom, calls=%fused_computation.2 | custom fusion | bytes 4724736 | tf_op jit(solution)/shard_map/gather | solution.py:105
  155.7 41.0 %all-gather.9.cloned.1.call-done = bf16[2048,512]{1,0:T(8,128)(2,1)} async-done(((bf16[64,512]{1,0:T(8,128)(2,1)}), bf16[2048,512]{1,0:T(8,128)(2,1)}) %all-gather.9.cloned.1.call-update) | async-done | bytes 2097168 | tf_op jit(solution)/shard_map/all_gather | solution.py:94
  196.7 2.3 %fusion.13 = f32[128,64]{0,1:T(8,128)S(1)} fusion(bf16[32,64,512]{2,1,0:T(8,128)(2,1)} %bitcast.183, f32[128,32]{0,1:T(8,128)S(1)} %bitcast_convert_fusion, bf16[128,512]{1,0:T(8,128)(2,1)S(1)} %copy-done.3), kind=kOutput, calls=%fused_computation.14 | convolution fusion | flops 268951552 | bytes 2277376 | tf_op jit(solution)/shard_map/ntk,bk->ntb/dot_general | solution.py:92
  199.1 0.1 convolution_bitcast_fusion.4
  199.2 0.1 reshape.267
  199.5 7.4 %fusion.10 = f32[6,6,16,256]{3,2,0,1:T(8,128)S(1)} fusion(f32[6,6,16,256]{3,2,0,1:T(8,128)S(1)} %convolution_bitcast_fusion.1, f32[6,64,6,256]{1,0,3,2:T(8,128)} %bitcast.175, f32[6,16,256]{2,1,0:T(8,128)S(1)} %pad.4, pred[6,256]{1,0:T(8,128)(4,1)S(1)} %broadcast_and_fusion, f32[6,16,64]{2,1,0:T(8,128)S(1)} %gather_fusion.3), kind=kOutput, calls=%fused_computation.13 | convolution fusion | flops 113541120 | bytes 3663360 | tf_op jit(solution)/shard_map/fqn,cnfe->fcqe/dot_general | solution.py:106
  206.9 1.1 fusion.19
  208.0 1.5 fusion.14
  (62 shorter events, 0.8 us)
Async XLA Ops:
  7.2 140.8 %copy-start = (f32[3,64,64]{2,1,0:T(8,128)S(1)}, f32[3,64,64]{2,1,0:T(8,128)}, u32[]{:S(2)}) copy-start(f32[3,64,64]{2,1,0:T(8,128)} %param.20) | copy-start | bytes 147460
  7.2 18.3 %copy-start.6 = (bf16[32,128]{1,0:T(8,128)(2,1)S(1)}, bf16[32,128]{1,0:T(8,128)(2,1)}, u32[]{:S(2)}) copy-start(bf16[32,128]{1,0:T(8,128)(2,1)} %param.30) | copy-start | bytes 24580
  7.2 100.9 %all-gather.7.cloned.1.call-start = ((), (), s32[]{:S(2)}) async-start(), calls=%async_computation.1 | async-start | bytes 4325376 | tf_op jit(solution)/shard_map/all_gather | solution.py:74
  7.9 188.8 %all-gather.9.cloned.1.call-start = ((), (), s32[]{:S(2)}) async-start(), calls=%async_computation.2 | async-start | bytes 2162688 | tf_op jit(solution)/shard_map/all_gather | solution.py:94
  111.3 29.8 %copy-start.13 = (s32[2,16]{1,0:T(2,128)S(1)}, s32[2,16]{1,0:T(2,128)}, u32[]{:S(2)}) copy-start(s32[2,16]{1,0:T(2,128)} %param.25) | copy-start | bytes 388
  111.3 30.0 %copy-start.1 = (f32[6,64,256]{2,1,0:T(8,128)S(1)}, f32[6,64,256]{2,1,0:T(8,128)}, u32[]{:S(2)}) copy-start(f32[6,64,256]{2,1,0:T(8,128)} %param.18) | copy-start | bytes 1179652
  111.3 36.6 %copy-start.8 = (s32[6,256]{1,0:T(8,128)S(1)}, s32[6,256]{1,0:T(8,128)}, u32[]{:S(2)}) copy-start(s32[6,256]{1,0:T(8,128)} %param.24) | copy-start | bytes 18436
  140.4 7.6 %copy-start.9 = (f32[256]{0:T(256)S(1)}, f32[256]{0:T(256)}, u32[]{:S(2)}) copy-start(f32[256]{0:T(256)} %param.19) | copy-start | bytes 3076
  141.7 7.5 %copy-start.12 = (s32[6]{0:T(128)S(1)}, s32[6]{0:T(128)}, u32[]{:S(2)}) copy-start(s32[6]{0:T(128)} %constant.80) | copy-start | bytes 76
  141.7 7.5 %copy-start.2 = (f32[6,16,64]{2,1,0:T(8,128)S(1)}, f32[6,16,64]{2,1,0:T(8,128)}, u32[]{:S(2)}) copy-start(f32[6,16,64]{2,1,0:T(8,128)} %param.21) | copy-start | bytes 73732
  142.5 7.3 %collective-permute-start = (bf16[6,64,16]{1,0,2:T(8,128)(2,1)S(1)}, bf16[6,64,16]{1,0,2:T(8,128)(2,1)S(1)}, u32[]{:S(2)}, u32[]{:S(2)}) collective-permute-start(bf16[6,64,16]{1,0,2:T(8,128)(2,1)S(1)} %get-tuple-element.9), channel_id=1, source_target_pairs={{0,1},{1,2},{2,3},{3,4},{4,5},{5,6},{6,7},{7,8},{8,9},{9,10},{10,1... | collective-permute-start | bytes 36872 | tf_op jit(solution)/shard_map/ppermute | solution.py:20
  142.6 7.3 %collective-permute-start.1 = (bf16[6,64,16]{1,0,2:T(8,128)(2,1)S(1)}, bf16[6,64,16]{1,0,2:T(8,128)(2,1)S(1)}, u32[]{:S(2)}, u32[]{:S(2)}) collective-permute-start(bf16[6,64,16]{1,0,2:T(8,128)(2,1)S(1)} %get-tuple-element.10), channel_id=1, source_target_pairs={{1,0},{2,1},{3,2},{4,3},{5,4},{6,5},{7,6},{8,7},{9,8},{10,9},{11,1... | collective-permute-start | bytes 36872 | tf_op jit(solution)/shard_map/ppermute | solution.py:21
  150.0 46.7 %copy-start.3 = (bf16[128,512]{1,0:T(8,128)(2,1)S(1)}, bf16[128,512]{1,0:T(8,128)(2,1)}, u32[]{:S(2)}) copy-start(bf16[128,512]{1,0:T(8,128)(2,1)} %param.31) | copy-start | bytes 393220
  155.7 43.3 %copy-start.10 = (f32[64]{0:T(128)S(1)}, f32[64]{0:T(128)}, u32[]{:S(2)}) copy-start(f32[64]{0:T(128)} %param.28) | copy-start | bytes 772
  155.7 43.7 %copy-start.11 = (f32[6]{0:T(128)S(1)}, f32[6]{0:T(128)}, u32[]{:S(2)}) copy-start(f32[6]{0:T(128)} %param.26) | copy-start | bytes 76
  199.1 7.8 %copy-start.4 = (f32[64,128]{1,0:T(8,128)}, f32[64,128]{1,0:T(8,128)S(1)}, u32[]{:S(2)}) copy-start(f32[64,128]{1,0:T(8,128)S(1)} %multiply_bitcast_fusion) | copy-start | bytes 98308
  199.5 7.4 %copy-start.7 = (f32[6,6,6]{2,1,0:T(8,128)S(1)}, f32[6,6,6]{2,1,0:T(8,128)}, u32[]{:S(2)}) copy-start(f32[6,6,6]{2,1,0:T(8,128)} %param.23) | copy-start | bytes 2596
  199.5 8.5 %copy-start.5 = (f32[6,64,16]{1,2,0:T(8,128)S(1)}, f32[6,64,16]{1,2,0:T(8,128)}, u32[]{:S(2)}) copy-start(f32[6,64,16]{1,2,0:T(8,128)} %param.22) | copy-start | bytes 73732
Sparse Core Ops, SparseCore 0:
  10.9 66.5 all-gather.6
  141.2 55.4 all-gather.8
where the time goes:
time: 217 us; the launch traced here: 216 us
  blocking collectives  112 us (52%)
  waiting for transfers between devices  41.7 us (19%)
  local copies, waits for them, and re-layouts  21.3 us (10%)
  matrix products  19.1 us (9%)
  between operations  15.1 us (7%)
  starting transfers between devices  5.46 us (3%)
    all_gather x1, blocking collectives, per_device(): lax.all_gather(group_weight[None], ('patch', 'level'), axis=0, tiled=True)  44.3 us
    all_gather x1, waiting for transfers between devices, per_device(): lax.all_gather(incoming[None], ('patch', 'level'), axis=0, tiled=True)  41 us
    all_gather x1, blocking collectives, per_device(): lax.all_gather(currents[None], ('patch', 'level'), axis=0, tiled=True)  38.2 us
    all_to_all x1, blocking collectives, per_device(): lax.all_to_all(blocks, 'patch', split_axis=0, concat_axis=0, tiled=True)  29.1 us
    gather x2, local copies, waits for them, and re-layouts, toeplitz(): picked = jnp.take(rows, jnp.clip(lagged, 0, count - 1), axis=-1)  12.5 us
    dot_general x1, matrix products, per_device(): neighbour = jnp.einsum('fqn,cnfe->fcqe', opposite, across, precision=HIGH)  7.37 us
    gather x1, local copies, waits for them, and re-layouts, per_device(): across = pool[:, :, neighbours]  5.7 us
    ppermute x1, starting transfers between devices, padded_2(): after = lax.ppermute(leading, axis, down)  5.33 us
  transfers between devices with their start and end apart: 4, of which 1 were waited for; matrix products, arithmetic and copies ran while one was open for 12% of the time, Pallas kernels for 0%

commit v1 on v0

v1 whole, which is shorter than its diff:
```python
import functools
import math

import jax
import jax.numpy as jnp
from jax import lax
from jax.experimental import pallas as pl
from jax.experimental.pallas import tpu as pltpu
from jax.sharding import PartitionSpec as P

MESH = pl.DeviceIdType.MESH
F32 = jnp.float32
BF16 = jnp.bfloat16
HIGH = lax.Precision.HIGHEST
COLUMNS = 2
CORES = 2


def iota(shape, dim):
    return lax.broadcasted_iota(jnp.int32, shape, dim)


def dot(a, b):
    return jnp.dot(a, b, preferred_element_type=F32)


def split(x):
    high = x.astype(BF16)
    return high, (x - high.astype(F32)).astype(BF16)


def one_hot(mask):
    return jnp.where(mask, 1.0, 0.0).astype(BF16)


def kernel(
    patches,
    levels,
    meta_rows,
    fields,
    scale,
    interp,
    diff,
    lift,
    couple,
    links,
    listed,
    bound_coef,
    current_coef,
    time_interp,
    history,
    weights,
    proj,
    kernels,
    dest,
    count,
    rate,
    boundary,
    pbuf,
    sbuf,
    sib_proj,
    sib_small,
    meta,
    outgoing,
    ghosts,
    pool,
    traces,
    grads,
    flux,
    rsum,
    gains,
    toep,
    gwf,
    partial,
    arrived,
    p_send,
    p_recv,
    s_send,
    s_recv,
    x_send,
    x_recv,
):
    depth = patches // COLUMNS
    wide = levels // CORES
    p, l = lax.axis_index("patch"), lax.axis_index("level")
    z, y = p // COLUMNS, p % COLUMNS
    x, core = l // CORES, l % CORES
    nt = history.shape[0]
    groups, nb = weights.shape
    pairs = kernels.shape[0]
    faces, nodes, elements = fields.shape
    halo = listed.shape[1]
    nq = interp.shape[0] // faces
    bound = nb // nq
    me = p * levels + l
    everyone = patches * levels

    def ident(flat):
        return (flat // levels, flat % levels)

    sibling = (p, x * CORES + (1 - core))
    after = ident((me + 1) % everyone)
    before = ident((me + everyone - 1) % everyone)
    ya, xa = (y + 1 - core) % COLUMNS, (x + core) % wide
    yb, xb = (y + core) % COLUMNS, (x + 1 - core) % wide
    near = (z * COLUMNS + ya, xa * CORES + core)
    far = (z * COLUMNS + yb, xb * CORES + core)

    def column(step):
        return ((z + step) % depth * COLUMNS + y, l)

    barrier = pltpu.get_barrier_semaphore()
    partners = [sibling, near, far, after, before] + [column(k) for k in range(1, depth)]
    for other in partners:
        pl.semaphore_signal(barrier, inc=1, device_id=other, device_id_type=MESH)

    mine = p * wide + x
    pbuf[mine] = proj[...]

    kr = dot(kernels[...], one_hot(iota((nt, 128), 0) + iota((nt, 128), 1) == nt - 1))
    row = iota((meta_rows, 128), 0)
    lane = iota((meta_rows, 128), 1)
    held = kr
    if meta_rows > pairs:
        held = jnp.concatenate([kr, jnp.zeros((meta_rows - pairs, 128), F32)], axis=0)
    goal = jnp.zeros((meta_rows, 128), F32)
    for j in range(pairs):
        goal = jnp.where(row == j, dest[j].astype(F32), goal)
    held = jnp.where(row < count[0], held, 0.0)
    meta[0:meta_rows] = jnp.where(lane < nt, held, goal).astype(BF16)
    meta[meta_rows:] = weights[...]

    mixed = current_coef[0] * fields[0, :, 0:128]
    for c in range(1, faces):
        mixed += current_coef[c] * fields[c, :, 0:128]
    last = jnp.dot(interp[nq * (faces - 1) :, :], mixed, precision=HIGH, preferred_element_type=F32)
    spread = jnp.where(iota((128, nb), 0) == iota((128, nb), 1) // nq, 1.0, 0.0)
    last = jnp.dot(last, spread, precision=HIGH, preferred_element_type=F32)
    diagonal = iota((nq, nb), 0) == iota((nq, nb), 1) % nq
    newest = jnp.sum(jnp.where(diagonal, last, 0.0), axis=0, keepdims=True)
    moved = pltpu.roll(history[...].astype(F32), nt - 1, 0)
    currents = jnp.where(iota((nt, nb), 0) == nt - 1, newest, moved).astype(BF16)
    sbuf[mine, 0:nt] = currents
    sbuf[mine, nt : nt + groups] = weights[...]
    base = nt + groups
    sbuf[mine, base : base + meta_rows] = meta[0:meta_rows]

    pl.semaphore_wait(barrier, len(partners))

    sends = []

    def send(src, dst, s_sem, r_sem, other):
        copy = pltpu.make_async_remote_copy(
            src_ref=src, dst_ref=dst, send_sem=s_sem, recv_sem=r_sem,
            device_id=other, device_id_type=MESH,
        )
        copy.start()
        sends.append(copy)
        return copy

    slots = [0, 0]

    def send_p(slot, other):
        i = slots[0]
        slots[0] += 1
        send(pbuf.at[slot], pbuf.at[slot], p_send.at[i], p_recv.at[slot], other)

    def send_s(slot, other):
        i = slots[1]
        slots[1] += 1
        send(sbuf.at[slot], sbuf.at[slot], s_send.at[i], s_recv.at[slot], other)

    def wait_p(slot):
        pltpu.make_async_copy(pbuf.at[slot], pbuf.at[slot], p_recv.at[slot]).wait()

    def wait_s(slot):
        pltpu.make_async_copy(sbuf.at[slot], sbuf.at[slot], s_recv.at[slot]).wait()

    sib_meta = send(meta, sib_small, x_send.at[0], x_recv.at[0], sibling)
    send_p(mine, far)
    send_p(mine, near)
    for k in range(1, depth):
        send_p(mine, column(k))
    sib_copy = send(proj, sib_proj, x_send.at[1], x_recv.at[1], sibling)

    place = jnp.where(iota((halo, 128), 0) == iota((halo, 128), 1) % halo, 1.0, 0.0)
    wanted = jnp.dot(listed[...].astype(F32), place, precision=HIGH, preferred_element_type=F32)
    wanted = wanted.astype(jnp.int32)
    picks = jnp.concatenate(
        [one_hot(iota((elements, 128), 0) == wanted[r : r + 1, :]) for r in range(2)], axis=1
    )
    sent = jnp.zeros((nodes, 256), F32)
    which = iota((nodes, 256), 1) % 128 // halo
    for c in range(faces):
        sent = jnp.where(which == c, dot(fields[c].astype(BF16), picks), sent)
    outgoing[0] = sent[:, 0:128].astype(BF16)
    outgoing[1] = sent[:, 128:256].astype(BF16)

    sib_meta.wait_recv()
    sbuf[mine, base + meta_rows : base + 2 * meta_rows] = sib_small[0:meta_rows]
    send_s(mine, far)
    send_s(mine, near)
    for k in range(1, depth):
        send_s(mine, column(k))
    up = send(outgoing.at[1], ghosts.at[0], x_send.at[2], x_recv.at[2], after)
    down = send(outgoing.at[0], ghosts.at[1], x_send.at[3], x_recv.at[3], before)

    rsum[...] = jnp.zeros_like(rsum)

    def slot_of(zz, yy, xx):
        return (zz * COLUMNS + yy) * wide + xx

    def prepare(slot):
        info = sbuf[slot, base : base + 2 * meta_rows].astype(F32)
        rows = iota((2 * meta_rows, groups), 0)
        theirs = jnp.where(rows < meta_rows, core, 1 - core)
        target = (info[:, nt : nt + 1].astype(jnp.int32)) * levels + slot % wide * CORES + theirs
        picked = one_hot(iota((2 * meta_rows, groups), 1) == target)
        both = jnp.concatenate([weights[...], sib_small[meta_rows:]], axis=1)
        gains[slot] = dot(picked, both)
        first = iota((nt, 128), 1) < nt
        for k in range(2):
            for j in range(0, pairs, 2):
                rolled = []
                for i in range(2):
                    r = k * meta_rows + j + i
                    line = jnp.where(iota((1, 128), 1) < nt, info[r : r + 1, :], 0.0)
                    line = jnp.broadcast_to(line, (nt, 128))
                    rolled.append(
                        pltpu.roll(line, (128 - nt + 1 + nt * i) % 128, 1, stride=1, stride_axis=0)
                    )
                at = (k * pairs + j) * nt
                toep[slot, :, at : at + 128] = jnp.where(first, rolled[0], rolled[1]).astype(BF16)

    def absorb(one, two):
        chip = jnp.concatenate([proj[...], sib_proj[...]], axis=0)
        both = []
        for i, slot in enumerate((one, two)):
            prepare(slot)
            s = lax.dot_general(
                pbuf[slot], chip, (((1,), (1,)), ((), ())), preferred_element_type=F32
            )
            both.append(s.astype(BF16))
            gwf[i] = sbuf[slot, nt : nt + groups].astype(F32)
        s = jnp.concatenate(both, axis=0)
        cur = [sbuf[slot, 0:nt].astype(F32) for slot in (one, two)]

        def chunk(i, carry):
            at = pl.multiple_of(i * 8, 8)
            w = [gwf[i2, pl.ds(at, 8), :] for i2 in range(2)]
            lhs = jnp.concatenate(
                [
                    jnp.concatenate(
                        [(cur[i2] * w[i2][g : g + 1, :]).astype(BF16) for i2 in range(2)], axis=1
                    )
                    for g in range(8)
                ],
                axis=0,
            )
            rows = pl.ds(pl.multiple_of(i * 8 * nt, 8 * nt), 8 * nt)
            rsum[rows, :] += dot(lhs, s)
            return carry

        lax.fori_loop(0, groups // 8, chunk, 0)

    home = [slot_of((z + depth - k) % depth, y, x) for k in range(depth)]
    for slot in home[1:]:
        wait_p(slot)
        send_p(slot, far)
        send_p(slot, near)
        wait_s(slot)
        send_s(slot, far)
        send_s(slot, near)

    up.wait_recv()
    down.wait_recv()
    arrivals = jnp.concatenate([ghosts[0], ghosts[1]], axis=1)
    r_i = iota((256, faces * 128), 0)
    m_i = iota((256, faces * 128), 1)
    lands = (r_i // 128 == m_i % 128 // halo) & (r_i % 128 == m_i // 128 * halo + m_i % halo)
    lands = one_hot(lands)
    unpacked = dot(arrivals, lands)
    width = elements + 128
    w_all = jnp.concatenate([interp[...], diff[...]], axis=0)
    w_hi, w_lo = split(w_all)
    w3 = jnp.concatenate([w_hi, w_hi, w_lo], axis=1)
    nf = faces * nq
    for c in range(faces):
        xc = jnp.concatenate([fields[c], unpacked[:, c * 128 : (c + 1) * 128]], axis=1)
        hi, lo = split(xc)
        got = dot(w3, jnp.concatenate([hi, lo, hi], axis=0))
        traces[c] = got[0:nf]
        grads[c] = got[nf:, 0:elements] * scale[...]

    nears = [slot_of((z + depth - k) % depth, ya, xa) for k in range(depth)]

    def forward(slot):
        wait_p(slot)
        send_p(slot, far)
        wait_s(slot)
        send_s(slot, far)

    todo = list(nears)
    lane_e = iota((nq, elements), 1)
    for f in range(faces):
        o = f + 1 - 2 * (f % 2)
        block = jnp.concatenate([traces[c, o * nq : (o + 1) * nq, :] for c in range(faces)], axis=0)
        hi, lo = split(block)
        pick = one_hot(iota((width, elements), 0) == links[f : f + 1, :])
        got = dot(jnp.concatenate([hi, lo], axis=0), pick)
        jump = []
        for c in range(faces):
            nbr = got[c * nq : (c + 1) * nq] + got[nf + c * nq : nf + (c + 1) * nq]
            if f == faces - 1:
                nbr = jnp.where(lane_e < bound, 0.0, nbr)
            jump.append(nbr - traces[c, f * nq : (f + 1) * nq, 0:elements])
        for c in range(faces):
            total = couple[(f * faces + c) * faces] * jump[0]
            for d in range(1, faces):
                total += couple[(f * faces + c) * faces + d] * jump[d]
            flux[c, f * nq : (f + 1) * nq, :] = total
    for slot in todo:
        forward(slot)

    sib_copy.wait_recv()
    l_hi = jnp.zeros((nodes, 128), F32)
    l_lo = jnp.zeros((nodes, 128), F32)
    for f in range(faces):
        hi, lo = split(lift[f])
        here = one_hot(iota((nq, 128), 1) == iota((nq, 128), 0) + f * nq)
        l_hi += dot(hi, here)
        l_lo += dot(lo, here)
    l_hi, l_lo = l_hi.astype(BF16), l_lo.astype(BF16)
    l3 = jnp.concatenate([l_hi, l_hi, l_lo], axis=1)
    empty = jnp.zeros((128 - nf, elements), BF16)
    for c in range(faces):
        hi, lo = split(flux[c])
        hi = jnp.concatenate([hi, empty], axis=0)
        lo = jnp.concatenate([lo, empty], axis=0)
        surface = dot(l3, jnp.concatenate([hi, lo, hi], axis=0))
        i, j = (c + 1) % 3, (c + 2) % 3
        other = 3 - c // 3 * 3

        def grad(r, d):
            return grads[d, r * nodes : (r + 1) * nodes, :]

        curl = grad(i, other + j) - grad(j, other + i)
        rate[c] = surface + curl if c < 3 else surface - curl

    for k in range(0, depth, 2):
        absorb(home[k], home[k + 1])
    for k in range(0, depth, 2):
        absorb(nears[k], nears[k + 1])
    ends = [slot_of((z + depth - k) % depth, yb, xb) for k in range(depth)]
    ends += [slot_of((z + depth - k) % depth, (y + 1) % COLUMNS, (x + 1) % wide) for k in range(depth)]
    for k in range(0, 2 * depth, 2):
        for slot in ends[k : k + 2]:
            wait_p(slot)
            wait_s(slot)
        absorb(ends[k], ends[k + 1])

    def finish(slot, total):
        parts = []
        for k in range(2):
            g = slot * 2 + (core if k == 0 else 1 - core)
            r = rsum[pl.ds(pl.multiple_of(g * nt, nt), nt), :]
            for j in range(pairs):
                gain = gains[slot, k * meta_rows + j : k * meta_rows + j + 1, :]
                parts.append((r * gain).astype(BF16))
        return total + dot(toep[slot], jnp.concatenate(parts, axis=0))

    total = lax.fori_loop(0, patches * wide, finish, jnp.zeros((nt, 2 * nb), F32))
    partial[...] = total[:, nb:]
    swap = send(partial, arrived, x_send.at[4], x_recv.at[4], sibling)
    swap.wait_recv()
    field = (total[:, 0:nb] + arrived[...]) * (1.0 / math.sqrt(proj.shape[1]))
    boundary[...] = field

    seen = jnp.dot(time_interp[...], field, precision=HIGH, preferred_element_type=F32)
    seen = jnp.where(diagonal, jnp.broadcast_to(seen, (nq, nb)), 0.0)
    gather = jnp.where(iota((nb, 128), 0) // nq == iota((nb, 128), 1), 1.0, 0.0)
    seen = jnp.dot(seen, gather, precision=HIGH, preferred_element_type=F32)
    added = jnp.dot(lift[faces - 1], seen, precision=HIGH, preferred_element_type=F32)
    for c in range(faces):
        factor = couple[((faces - 1) * faces + c) * faces] * bound_coef[0]
        for d in range(1, faces):
            factor += couple[((faces - 1) * faces + c) * faces + d] * bound_coef[d]
        rate[c, :, 0:128] += factor * added

    for copy in sends:
        copy.wait_send()


def per_device(
    fields, inv_jacobian, diff_matrix, face_interp, lift_matrix, flux_couple, neighbours,
    send_index, bound_coef, current_coef, time_interp, current_history, group_weight,
    projection, kernels, pair_dest, pair_count,
):
    patches, levels = lax.axis_size("patch"), lax.axis_size("level")
    faces, nodes, elements = fields.shape
    nt, nb = current_history.shape
    groups = group_weight.shape[0]
    ndir = projection.shape[1]
    pairs = kernels.shape[2]
    meta_rows = -(-pairs // 16) * 16
    nq = face_interp.shape[1]
    chips = patches * (levels // CORES)
    depth = patches // COLUMNS
    n_send = 4 * depth - 1
    rows = nt + groups + 2 * meta_rows
    vmem = pl.BlockSpec(memory_space=pltpu.VMEM)
    smem = pl.BlockSpec(memory_space=pltpu.SMEM)
    dma = pltpu.SemaphoreType.DMA
    return pl.pallas_call(
        functools.partial(kernel, patches, levels, meta_rows),
        out_shape=(
            jax.ShapeDtypeStruct(fields.shape, F32),
            jax.ShapeDtypeStruct((nt, nb), F32),
        ),
        in_specs=[vmem] * 5 + [smem] + [vmem] * 2 + [smem] * 2 + [vmem] * 5 + [smem] * 2,
        out_specs=(vmem, vmem),
        scratch_shapes=[
            pltpu.VMEM((chips, nb, ndir), BF16),
            pltpu.VMEM((chips, rows, nb), BF16),
            pltpu.VMEM((nb, ndir), BF16),
            pltpu.VMEM((meta_rows + groups, nb), BF16),
            pltpu.VMEM((meta_rows + groups, nb), BF16),
            pltpu.VMEM((2, nodes, 128), BF16),
            pltpu.VMEM((2, nodes, 128), BF16),
            pltpu.VMEM((8, 128), F32),
            pltpu.VMEM((faces, faces * nq, elements + 128), F32),
            pltpu.VMEM((faces, 3 * nodes, elements), F32),
            pltpu.VMEM((faces, faces * nq, elements), F32),
            pltpu.VMEM((groups * nt, 2 * nb), F32),
            pltpu.VMEM((chips, 2 * meta_rows, 2 * nb), F32),
            pltpu.VMEM((chips, nt, 2 * pairs * nt), BF16),
            pltpu.VMEM((2, groups, nb), F32),
            pltpu.VMEM((nt, nb), F32),
            pltpu.VMEM((nt, nb), F32),
            dma((n_send,)),
            dma((chips,)),
            dma((n_send,)),
            dma((chips,)),
            dma((5,)),
            dma((5,)),
        ],
        compiler_params=pltpu.CompilerParams(
            collective_id=0, has_side_effects=True, vmem_limit_bytes=56 * 1024 * 1024
        ),
    )(
        fields,
        inv_jacobian.reshape(1, elements),
        face_interp.reshape(faces * nq, nodes),
        diff_matrix.reshape(3 * nodes, nodes),
        lift_matrix,
        flux_couple.reshape(-1),
        neighbours,
        send_index,
        bound_coef,
        current_coef,
        time_interp.reshape(1, nt),
        current_history,
        group_weight,
        projection,
        kernels.reshape(pairs, nt),
        pair_dest.reshape(pairs),
        pair_count.reshape(1),
    )


def solution(mesh):
    both = ("patch", "level")
    placed = (
        P(None, None, both),
        P(both),
        P(),
        P(),
        P(),
        P(),
        P(None, both),
        P(None, both),
        P(),
        P(),
        P(),
        P(None, both),
        P(None, both),
        P(both, None),
        P("level", "patch", None, None),
        P("level", "patch", None),
        P("level", "patch"),
    )
    return jax.shard_map(
        per_device,
        mesh=mesh,
        in_specs=placed,
        out_specs=(P(None, None, both), P(None, both)),
        check_vma=False,
    )
```

time: 217 us -> 53.7 us (0.25)
  the two profiles are of different devices: /device:TPU:0 before, /device:TPU:19 now
where the time goes in v1:
time: 53.7 us; the launch traced here: 53.4 us
  Pallas kernels  46.7 us (87%)
  local copies, waits for them, and re-layouts  5.4 us (10%)
  between operations  1.29 us (2%)
    pallas_call x1, Pallas kernels, per_device(): pl.pallas_call(functools.partial(kernel, patches, levels, meta_rows), out...  46.7 us
    unnamed x5, local copies, waits for them, and re-layouts  3.99 us
    reshape x1, local copies, waits for them, and re-layouts, per_device(): flux_couple.reshape(-1)  1.41 us

profile of v1, /device:TPU:19, one launch (start us, length us, event | category | flops | bytes accessed | tf_op | source)
XLA Modules:
  0.0 53.4 jit_solution(18436495278074134228)
XLA Ops:
  1.3 1.4 %reshape.31.couple = f32[216]{0:T(256)} reshape(f32[6,6,6]{2,1,0:T(8,128)} %param.22) | data formatting | bytes 1728 | tf_op jit(solution)/shard_map/reshape | solution.py:456
  2.7 1.6 %copy.19.lift = f32[6,64,16]{2,1,0:T(8,128)} copy(f32[6,64,16]{1,2,0:T(8,128)} %param.21) | data formatting | bytes 49152 | tf_op args[4]
  4.3 46.7 %shard_map.176 = (f32[6,64,256]{2,1,0:T(8,128)}, f32[64,128]{1,0:T(8,128)}) custom-call(f32[6,64,256]{2,1,0:T(8,128)} %fields.1, f32[1,256]{1,0:T(1,128)} %bitcast.10, f32[96,64]{1,0:T(8,128)} %bitcast.9, f32[192,64]{1,0:T(8,128)} %bitcast.8, f32[6,64,16]{2,1,0:T(8,128)} %copy.19.lift, f32[216]{0:T(256)} %reshape.31.couple, s32[6,256]{1,0:T(8,128)} %links.1, ...), custom_call_target="tpu_custom_call" | custom-call | tf_op jit(solution)/shard_map/pallas_call | solution.py:414
  51.0 0.0 copy-start
  51.0 1.8 %copy.23 = f32[6,64,256]{2,1,0:T(8,128)} copy(f32[6,64,256]{2,1,0:T(8,128)} %get-tuple-element.4) | data formatting | bytes 786432
  52.8 0.0 copy-done
  52.8 0.6 %copy.24 = f32[64,128]{1,0:T(8,128)} copy(f32[64,128]{1,0:T(8,128)S(1)} %copy-done) | data formatting | bytes 65536
Async XLA Ops:
  51.0 1.8 %copy-start = (f32[64,128]{1,0:T(8,128)S(1)}, f32[64,128]{1,0:T(8,128)}, u32[]{:S(2)}) copy-start(f32[64,128]{1,0:T(8,128)} %get-tuple-element.5) | copy-start | bytes 98308

commit v2 on v1

--- a/solution.py
+++ b/solution.py
@@ -58,7 +58,7 @@
     boundary,
     pbuf,
     sbuf,
-    sib_proj,
+    chip,
     sib_small,
     meta,
     outgoing,
@@ -106,16 +106,77 @@
     near = (z * COLUMNS + ya, xa * CORES + core)
     far = (z * COLUMNS + yb, xb * CORES + core)
 
-    def column(step):
-        return ((z + step) % depth * COLUMNS + y, l)
+    above = ((z + 1) % depth * COLUMNS + y, l)
+    below = ((z + depth - 1) % depth * COLUMNS + y, l)
+    has_above, has_below = z < depth - 1, z > 0
 
     barrier = pltpu.get_barrier_semaphore()
-    partners = [sibling, near, far, after, before] + [column(k) for k in range(1, depth)]
+
+    def greet(other):
+        pl.semaphore_signal(barrier, inc=1, device_id=other, device_id_type=MESH)
+
+    partners = [sibling, near, far, after, before, above, below]
     for other in partners:
-        pl.semaphore_signal(barrier, inc=1, device_id=other, device_id_type=MESH)
+        greet(other)
+    pl.semaphore_wait(barrier, len(partners))
+
+    sends = []
+
+    def remote(src, dst, s_sem, r_sem, other):
+        return pltpu.make_async_remote_copy(
+            src_ref=src, dst_ref=dst, send_sem=s_sem, recv_sem=r_sem,
+            device_id=other, device_id_type=MESH,
+        )
+
+    def send(*args):
+        copy = remote(*args)
+        copy.start()
+        sends.append(copy)
+        return copy
 
     mine = p * wide + x
-    pbuf[mine] = proj[...]
+
+    def slot_of(zz, yy, xx):
+        return (zz * COLUMNS + yy) * wide + xx
+
+    def hop(kind, slot, i, other, own=False):
+        buf, s_sem, r_sem = (pbuf, p_send, p_recv) if kind == "p" else (sbuf, s_send, s_recv)
+        src = proj if own and kind == "p" else buf.at[slot]
+        return remote(src, buf.at[slot], s_sem.at[i], r_sem.at[slot], other)
+
+    def wait(kind, slot):
+        buf, r_sem = (pbuf, p_recv) if kind == "p" else (sbuf, s_recv)
+        pltpu.make_async_copy(buf.at[slot], buf.at[slot], r_sem.at[slot]).wait()
+
+    def hops(kind, zz, k, side, act):
+        slot = slot_of(zz, y, x)
+        own = k == 0
+        if own or side == "below":
+            pl.when(has_above)(lambda: act(hop(kind, slot, 3 * depth + k, above, own)))
+        if own or side == "above":
+            pl.when(has_below)(lambda: act(hop(kind, slot, 4 * depth + k, below, own)))
+        act(hop(kind, slot, depth + zz, far, own))
+        act(hop(kind, slot, zz, near, own))
+
+    def start(copy):
+        copy.start()
+
+    def chain(kind, k, act, receive):
+        def from_below():
+            if receive:
+                wait(kind, slot_of(z - k, y, x))
+            hops(kind, z - k, k, "below", act)
+
+        def from_above():
+            if receive:
+                wait(kind, slot_of(z + k, y, x))
+            hops(kind, z + k, k, "above", act)
+
+        pl.when(z >= k)(from_below)
+        pl.when(z + k < depth)(from_above)
+
+    hops("p", z, 0, "", start)
+    sib_copy = send(proj, chip.at[1], x_send.at[1], x_recv.at[1], sibling)
 
     kr = dot(kernels[...], one_hot(iota((nt, 128), 0) + iota((nt, 128), 1) == nt - 1))
     row = iota((meta_rows, 128), 0)
@@ -126,10 +187,11 @@
     goal = jnp.zeros((meta_rows, 128), F32)
     for j in range(pairs):
         goal = jnp.where(row == j, dest[j].astype(F32), goal)
-    held = jnp.where(row < count[0], held, 0.0)
+    held = jnp.where(row < count[0, 0], held, 0.0)
     meta[0:meta_rows] = jnp.where(lane < nt, held, goal).astype(BF16)
     meta[meta_rows:] = weights[...]
 
+    sib_meta = send(meta, sib_small, x_send.at[0], x_recv.at[0], sibling)
     mixed = current_coef[0] * fields[0, :, 0:128]
     for c in range(1, faces):
         mixed += current_coef[c] * fields[c, :, 0:128]
@@ -145,44 +207,6 @@
     base = nt + groups
     sbuf[mine, base : base + meta_rows] = meta[0:meta_rows]
 
-    pl.semaphore_wait(barrier, len(partners))
-
-    sends = []
-
-    def send(src, dst, s_sem, r_sem, other):
-        copy = pltpu.make_async_remote_copy(
-            src_ref=src, dst_ref=dst, send_sem=s_sem, recv_sem=r_sem,
-            device_id=other, device_id_type=MESH,
-        )
-        copy.start()
-        sends.append(copy)
-        return copy
-
-    slots = [0, 0]
-
-    def send_p(slot, other):
-        i = slots[0]
-        slots[0] += 1
-        send(pbuf.at[slot], pbuf.at[slot], p_send.at[i], p_recv.at[slot], other)
-
-    def send_s(slot, other):
-        i = slots[1]
-        slots[1] += 1
-        send(sbuf.at[slot], sbuf.at[slot], s_send.at[i], s_recv.at[slot], other)
-
-    def wait_p(slot):
-        pltpu.make_async_copy(pbuf.at[slot], pbuf.at[slot], p_recv.at[slot]).wait()
-
-    def wait_s(slot):
-        pltpu.make_async_copy(sbuf.at[slot], sbuf.at[slot], s_recv.at[slot]).wait()
-
-    sib_meta = send(meta, sib_small, x_send.at[0], x_recv.at[0], sibling)
-    send_p(mine, far)
-    send_p(mine, near)
-    for k in range(1, depth):
-        send_p(mine, column(k))
-    sib_copy = send(proj, sib_proj, x_send.at[1], x_recv.at[1], sibling)
-
     place = jnp.where(iota((halo, 128), 0) == iota((halo, 128), 1) % halo, 1.0, 0.0)
     wanted = jnp.dot(listed[...].astype(F32), place, precision=HIGH, preferred_element_type=F32)
     wanted = wanted.astype(jnp.int32)
@@ -198,17 +222,13 @@
 
     sib_meta.wait_recv()
     sbuf[mine, base + meta_rows : base + 2 * meta_rows] = sib_small[0:meta_rows]
-    send_s(mine, far)
-    send_s(mine, near)
-    for k in range(1, depth):
-        send_s(mine, column(k))
+    hops("s", z, 0, "", start)
     up = send(outgoing.at[1], ghosts.at[0], x_send.at[2], x_recv.at[2], after)
     down = send(outgoing.at[0], ghosts.at[1], x_send.at[3], x_recv.at[3], before)
 
+    pbuf[mine] = proj[...]
+    chip[0] = proj[...]
     rsum[...] = jnp.zeros_like(rsum)
-
-    def slot_of(zz, yy, xx):
-        return (zz * COLUMNS + yy) * wide + xx
 
     def prepare(slot):
         info = sbuf[slot, base : base + 2 * meta_rows].astype(F32)
@@ -232,26 +252,26 @@
                 at = (k * pairs + j) * nt
                 toep[slot, :, at : at + 128] = jnp.where(first, rolled[0], rolled[1]).astype(BF16)
 
-    def absorb(one, two):
-        chip = jnp.concatenate([proj[...], sib_proj[...]], axis=0)
-        both = []
-        for i, slot in enumerate((one, two)):
+    def absorb(slots):
+        n = len(slots)
+        for i, slot in enumerate(slots):
             prepare(slot)
-            s = lax.dot_general(
-                pbuf[slot], chip, (((1,), (1,)), ((), ())), preferred_element_type=F32
-            )
-            both.append(s.astype(BF16))
             gwf[i] = sbuf[slot, nt : nt + groups].astype(F32)
-        s = jnp.concatenate(both, axis=0)
-        cur = [sbuf[slot, 0:nt].astype(F32) for slot in (one, two)]
+        s = lax.dot_general(
+            jnp.concatenate([pbuf[slot] for slot in slots], axis=0),
+            chip[...].reshape(2 * nb, proj.shape[1]),
+            (((1,), (1,)), ((), ())),
+            preferred_element_type=F32,
+        ).astype(BF16)
+        cur = [sbuf[slot, 0:nt].astype(F32) for slot in slots]
 
         def chunk(i, carry):
             at = pl.multiple_of(i * 8, 8)
-            w = [gwf[i2, pl.ds(at, 8), :] for i2 in range(2)]
+            w = [gwf[j, pl.ds(at, 8), :] for j in range(n)]
             lhs = jnp.concatenate(
                 [
                     jnp.concatenate(
-                        [(cur[i2] * w[i2][g : g + 1, :]).astype(BF16) for i2 in range(2)], axis=1
+                        [(cur[j] * w[j][g : g + 1, :]).astype(BF16) for j in range(n)], axis=1
                     )
                     for g in range(8)
                 ],
@@ -264,13 +284,18 @@
         lax.fori_loop(0, groups // 8, chunk, 0)
 
     home = [slot_of((z + depth - k) % depth, y, x) for k in range(depth)]
-    for slot in home[1:]:
-        wait_p(slot)
-        send_p(slot, far)
-        send_p(slot, near)
-        wait_s(slot)
-        send_s(slot, far)
-        send_s(slot, near)
+    nears = [slot_of((z + depth - k) % depth, ya, xa) for k in range(depth)]
+    half = depth // 2
+
+    def forward(k):
+        for kind in ("p", "s"):
+            wait(kind, nears[k])
+            hop(kind, nears[k], 2 * depth + k, far).start()
+
+    for k in range(1, depth):
+        chain("p", k, start, True)
+        chain("s", k, start, True)
+    forward(0)
 
     up.wait_recv()
     down.wait_recv()
@@ -292,15 +317,6 @@
         traces[c] = got[0:nf]
         grads[c] = got[nf:, 0:elements] * scale[...]
 
-    nears = [slot_of((z + depth - k) % depth, ya, xa) for k in range(depth)]
-
-    def forward(slot):
-        wait_p(slot)
-        send_p(slot, far)
-        wait_s(slot)
-        send_s(slot, far)
-
-    todo = list(nears)
     lane_e = iota((nq, elements), 1)
     for f in range(faces):
         o = f + 1 - 2 * (f % 2)
@@ -315,22 +331,15 @@
                 nbr = jnp.where(lane_e < bound, 0.0, nbr)
             jump.append(nbr - traces[c, f * nq : (f + 1) * nq, 0:elements])
         for c in range(faces):
-            total = couple[(f * faces + c) * faces] * jump[0]
+            total = couple[f, c : c + 1, 0:1] * jump[0]
             for d in range(1, faces):
-                total += couple[(f * faces + c) * faces + d] * jump[d]
+                total += couple[f, c : c + 1, d : d + 1] * jump[d]
             flux[c, f * nq : (f + 1) * nq, :] = total
-    for slot in todo:
-        forward(slot)
-
+    for k in range(1, half):
+        forward(k)
     sib_copy.wait_recv()
-    l_hi = jnp.zeros((nodes, 128), F32)
-    l_lo = jnp.zeros((nodes, 128), F32)
-    for f in range(faces):
-        hi, lo = split(lift[f])
-        here = one_hot(iota((nq, 128), 1) == iota((nq, 128), 0) + f * nq)
-        l_hi += dot(hi, here)
-        l_lo += dot(lo, here)
-    l_hi, l_lo = l_hi.astype(BF16), l_lo.astype(BF16)
+    flat = jnp.concatenate([lift[...].reshape(nf, nodes), jnp.zeros((128 - nf, nodes), F32)], axis=0)
+    l_hi, l_lo = split(flat.T)
     l3 = jnp.concatenate([l_hi, l_hi, l_lo], axis=1)
     empty = jnp.zeros((128 - nf, elements), BF16)
     for c in range(faces):
@@ -347,17 +356,25 @@
         curl = grad(i, other + j) - grad(j, other + i)
         rate[c] = surface + curl if c < 3 else surface - curl
 
+    def some(slots, width):
+        for k in range(0, len(slots), width):
+            absorb(slots[k : k + width])
+
+    some(home, 4)
+    for k in range(half, depth):
+        forward(k)
+    some(nears, 4)
+    ends = [slot_of((z + depth - k) % depth, yb, xb) for k in range(depth)]
+    for slot in ends:
+        wait("p", slot)
+        wait("s", slot)
+    some(ends, 4)
+    ends = [slot_of((z + depth - k) % depth, (y + 1) % COLUMNS, (x + 1) % wide) for k in range(depth)]
     for k in range(0, depth, 2):
-        absorb(home[k], home[k + 1])
-    for k in range(0, depth, 2):
-        absorb(nears[k], nears[k + 1])
-    ends = [slot_of((z + depth - k) % depth, yb, xb) for k in range(depth)]
-    ends += [slot_of((z + depth - k) % depth, (y + 1) % COLUMNS, (x + 1) % wide) for k in range(depth)]
-    for k in range(0, 2 * depth, 2):
         for slot in ends[k : k + 2]:
-            wait_p(slot)
-            wait_s(slot)
-        absorb(ends[k], ends[k + 1])
+            wait("p", slot)
+            wait("s", slot)
+        absorb(ends[k : k + 2])
 
     def finish(slot, total):
         parts = []
@@ -369,7 +386,7 @@
                 parts.append((r * gain).astype(BF16))
         return total + dot(toep[slot], jnp.concatenate(parts, axis=0))
 
-    total = lax.fori_loop(0, patches * wide, finish, jnp.zeros((nt, 2 * nb), F32))
+    total = lax.fori_loop(0, patches * wide, finish, jnp.zeros((nt, 2 * nb), F32), unroll=4)
     partial[...] = total[:, nb:]
     swap = send(partial, arrived, x_send.at[4], x_recv.at[4], sibling)
     swap.wait_recv()
@@ -380,15 +397,25 @@
     seen = jnp.where(diagonal, jnp.broadcast_to(seen, (nq, nb)), 0.0)
     gather = jnp.where(iota((nb, 128), 0) // nq == iota((nb, 128), 1), 1.0, 0.0)
     seen = jnp.dot(seen, gather, precision=HIGH, preferred_element_type=F32)
-    added = jnp.dot(lift[faces - 1], seen, precision=HIGH, preferred_element_type=F32)
+    added = jnp.dot(lift[faces - 1].T, seen, precision=HIGH, preferred_element_type=F32)
     for c in range(faces):
-        factor = couple[((faces - 1) * faces + c) * faces] * bound_coef[0]
+        factor = couple[faces - 1, c : c + 1, 0:1] * bound_coef[0]
         for d in range(1, faces):
-            factor += couple[((faces - 1) * faces + c) * faces + d] * bound_coef[d]
+            factor += couple[faces - 1, c : c + 1, d : d + 1] * bound_coef[d]
         rate[c, :, 0:128] += factor * added
 
     for copy in sends:
         copy.wait_send()
+
+    def sent_off(copy):
+        copy.wait_send()
+
+    for kind in ("p", "s"):
+        hops(kind, z, 0, "", sent_off)
+        for k in range(1, depth):
+            chain(kind, k, sent_off, False)
+        for k in range(depth):
+            hop(kind, nears[k], 2 * depth + k, far).wait_send()
 
 
 def per_device(
@@ -406,7 +433,7 @@
     nq = face_interp.shape[1]
     chips = patches * (levels // CORES)
     depth = patches // COLUMNS
-    n_send = 4 * depth - 1
+    n_send = 5 * depth
     rows = nt + groups + 2 * meta_rows
     vmem = pl.BlockSpec(memory_space=pltpu.VMEM)
     smem = pl.BlockSpec(memory_space=pltpu.SMEM)
@@ -417,12 +444,12 @@
             jax.ShapeDtypeStruct(fields.shape, F32),
             jax.ShapeDtypeStruct((nt, nb), F32),
         ),
-        in_specs=[vmem] * 5 + [smem] + [vmem] * 2 + [smem] * 2 + [vmem] * 5 + [smem] * 2,
+        in_specs=[vmem] * 8 + [smem] * 2 + [vmem] * 5 + [smem] * 2,
         out_specs=(vmem, vmem),
         scratch_shapes=[
             pltpu.VMEM((chips, nb, ndir), BF16),
             pltpu.VMEM((chips, rows, nb), BF16),
-            pltpu.VMEM((nb, ndir), BF16),
+            pltpu.VMEM((2, nb, ndir), BF16),
             pltpu.VMEM((meta_rows + groups, nb), BF16),
             pltpu.VMEM((meta_rows + groups, nb), BF16),
             pltpu.VMEM((2, nodes, 128), BF16),
@@ -434,7 +461,7 @@
             pltpu.VMEM((groups * nt, 2 * nb), F32),
             pltpu.VMEM((chips, 2 * meta_rows, 2 * nb), F32),
             pltpu.VMEM((chips, nt, 2 * pairs * nt), BF16),
-            pltpu.VMEM((2, groups, nb), F32),
+            pltpu.VMEM((4, groups, nb), F32),
             pltpu.VMEM((nt, nb), F32),
             pltpu.VMEM((nt, nb), F32),
             dma((n_send,)),
@@ -452,8 +479,8 @@
         inv_jacobian.reshape(1, elements),
         face_interp.reshape(faces * nq, nodes),
         diff_matrix.reshape(3 * nodes, nodes),
-        lift_matrix,
-        flux_couple.reshape(-1),
+        lift_matrix.transpose(0, 2, 1),
+        flux_couple,
         neighbours,
         send_index,
         bound_coef,
@@ -464,7 +491,7 @@
         projection,
         kernels.reshape(pairs, nt),
         pair_dest.reshape(pairs),
-        pair_count.reshape(1),
+        pair_count,
     )
 
 

time: 53.7 us -> 43.6 us (0.81)
  the two profiles are of different devices: /device:TPU:19 before, /device:TPU:0 now
where the time goes in v2:
time: 43.6 us; the launch traced here: 43 us
  Pallas kernels  39.3 us (90%)
  local copies, waits for them, and re-layouts  2.4 us (6%)
  between operations  1.3 us (3%)
    pallas_call x1, Pallas kernels, per_device(): pl.pallas_call(functools.partial(kernel, patches, levels, meta_rows), out...  39.3 us
    unnamed x4, local copies, waits for them, and re-layouts  2.4 us

profile of v2, /device:TPU:0, one launch (start us, length us, event | category | flops | bytes accessed | tf_op | source)
XLA Modules:
  0.0 43.0 jit_solution(10233163026874793308)
XLA Ops:
  1.3 39.3 %shard_map.176 = (f32[6,64,256]{2,1,0:T(8,128)}, f32[64,128]{1,0:T(8,128)}) custom-call(f32[6,64,256]{2,1,0:T(8,128)} %fields.1, f32[1,256]{1,0:T(1,128)} %bitcast.10, f32[96,64]{1,0:T(8,128)} %bitcast.8, f32[192,64]{1,0:T(8,128)} %bitcast.7, f32[6,16,64]{2,1,0:T(8,128)} %bitcast.9, f32[6,6,6]{2,1,0:T(8,128)} %couple.1, s32[6,256]{1,0:T(8,128)} %links.1, ...), custom_call_target="tpu_custom_call" | custom-call | tf_op jit(solution)/shard_map/pallas_call | solution.py:441
  40.6 0.0 copy-start
  40.6 1.8 %copy.22 = f32[6,64,256]{2,1,0:T(8,128)} copy(f32[6,64,256]{2,1,0:T(8,128)} %get-tuple-element.4) | data formatting | bytes 786432
  42.4 0.0 copy-done
  42.4 0.6 %copy.23 = f32[64,128]{1,0:T(8,128)} copy(f32[64,128]{1,0:T(8,128)S(1)} %copy-done) | data formatting | bytes 65536
Async XLA Ops:
  40.6 1.8 %copy-start = (f32[64,128]{1,0:T(8,128)S(1)}, f32[64,128]{1,0:T(8,128)}, u32[]{:S(2)}) copy-start(f32[64,128]{1,0:T(8,128)} %get-tuple-element.5) | copy-start | bytes 98308
